TPU v7x, 32 devices: a whole 2x2x4 slice. The times are simulated.
32 devices in a mesh: dp: 4 (over y, x), fsdp: 8 (over z, core).
Axes of the slice: x: 2, y: 2, z: 4, core: 2. Of those that a mesh axis runs over, the one named last changes fastest.
Arguments:
- inputs: float32 [32, 197, 768], P(('dp', 'fsdp')), may hold values from -6 to 6
- cotangent: float32 [32, 197, 768], P(('dp', 'fsdp')), may hold values from -6 to 6
- counts: int32 [32], P(('dp', 'fsdp')), may hold values from 0 to 1, as said below
- qkv_weight: float32 [1769472], P(('dp', 'fsdp')), may hold values from -0.21875 to 0.21875
- proj_weight: float32 [589824], P(('dp', 'fsdp')), may hold values from -0.875 to 0.875
- up_weight: float32 [2359296], P(('dp', 'fsdp')), may hold values from -0.21875 to 0.21875
- down_weight: float32 [2359296], P(('dp', 'fsdp')), may hold values from -0.109375 to 0.109375
- vectors: float32 [9216], P(('dp', 'fsdp')), may hold values from -2 to 2
- qkv_moment: float32 [1769472], P(('dp', 'fsdp')), may hold values from -18 to 18
- proj_moment: float32 [589824], P(('dp', 'fsdp')), may hold values from -18 to 18
- up_moment: float32 [2359296], P(('dp', 'fsdp')), may hold values from -18 to 18
- down_moment: float32 [2359296], P(('dp', 'fsdp')), may hold values from -18 to 18
- vectors_moment: float32 [9216], P(('dp', 'fsdp')), may hold values from -18 to 18
- qkv_square: float32 [1769472], P(('dp', 'fsdp')), may hold values from 6.304 to 25.216
- proj_square: float32 [589824], P(('dp', 'fsdp')), may hold values from 1.13472 to 4.53888
- up_square: float32 [2359296], P(('dp', 'fsdp')), may hold values from 0.37824 to 1.51296
- down_square: float32 [2359296], P(('dp', 'fsdp')), may hold values from 1.13472 to 4.53888
- vectors_square: float32 [9216], P(('dp', 'fsdp')), may hold values from 3.152 to 12.608
Outputs:
- block_out: float32 [32, 197, 768], P(('dp', 'fsdp'))
- input_grad: float32 [32, 197, 768], P(('dp', 'fsdp'))
- qkv_grad: float32 [1769472], P(('dp', 'fsdp'))
- proj_grad: float32 [589824], P(('dp', 'fsdp'))
- up_grad: float32 [2359296], P(('dp', 'fsdp'))
- down_grad: float32 [2359296], P(('dp', 'fsdp'))
- vectors_grad: float32 [9216], P(('dp', 'fsdp'))
- qkv_updated: float32 [1769472], P(('dp', 'fsdp'))
- proj_updated: float32 [589824], P(('dp', 'fsdp'))
- up_updated: float32 [2359296], P(('dp', 'fsdp'))
- down_updated: float32 [2359296], P(('dp', 'fsdp'))
- vectors_change: float32 [9216], P(('dp', 'fsdp'))
- qkv_moment_new: float32 [1769472], P(('dp', 'fsdp'))
- proj_moment_new: float32 [589824], P(('dp', 'fsdp'))
- up_moment_new: float32 [2359296], P(('dp', 'fsdp'))
- down_moment_new: float32 [2359296], P(('dp', 'fsdp'))
- vectors_moment_new: float32 [9216], P(('dp', 'fsdp'))
- qkv_square_new: float32 [1769472], P(('dp', 'fsdp'))
- proj_square_new: float32 [589824], P(('dp', 'fsdp'))
- up_square_new: float32 [2359296], P(('dp', 'fsdp'))
- down_square_new: float32 [2359296], P(('dp', 'fsdp'))
- vectors_square_new: float32 [9216], P(('dp', 'fsdp'))
Inputs may be any that keep to these rules, and one draw needn't show every extreme that they name: `counts`: the number of live image slots of each device, the live ones first; some device has all 1 live.
All inputs are finite; a program needn't handle non-finite values.
Results may differ from a plain program's by a relative error of at most 0.011.
Values may be sent and summed in bfloat16 or wider, within the bound.
A program may use at most 192 MiB of HBM per device.

v0:
```python
import math

import jax
import jax.numpy as jnp
from jax import lax
from jax.sharding import PartitionSpec as P

D = 768
HEADS = 12
HD = 64
FF = 3072


norm_eps = 1e-06
beta_first = 0.9
beta_second = 0.999
adam_eps = 1e-08
learn_rate = 0.02
weight_decay = 0.05


def as_sent(shard):

    def short(part):
        return part.astype(jnp.bfloat16) if part.dtype == jnp.float32 else part

    return jax.tree.map(short, shard)


def norm_stats(values):
    row_mean = jnp.mean(values, axis=-1, keepdims=True)
    centered = values - row_mean
    inverse = lax.rsqrt(jnp.mean(centered * centered, axis=-1, keepdims=True) + norm_eps)
    return (centered * inverse, inverse)


def norm_back(grad_normed, normed, inverse):
    first_mean = jnp.mean(grad_normed, axis=-1, keepdims=True)
    second_mean = jnp.mean(grad_normed * normed, axis=-1, keepdims=True)
    return inverse * (grad_normed - first_mean - normed * second_mean)


def gelu_parts(pre_act):
    normal_cdf = 0.5 * (1.0 + lax.erf(pre_act * 0.7071067811865476))
    normal_pdf = jnp.exp(-0.5 * pre_act * pre_act) * 0.3989422804014327
    return (pre_act * normal_cdf, normal_cdf + pre_act * normal_pdf)


def split_vectors(vector_values):
    pieces = []
    for position in range(7):
        pieces.append(vector_values[position * D : (position + 1) * D])
    pieces.append(vector_values[7 * D : 7 * D + FF])
    pieces.append(vector_values[7 * D + FF : 8 * D + FF])
    return pieces


def mixed_dot(left_side, right_side):
    return jnp.dot(left_side, right_side, preferred_element_type=jnp.float32)


def low_einsum(form, left_side, right_side):
    return jnp.einsum(form, left_side, right_side, preferred_element_type=jnp.float32)


def outer_sum(left_side, right_side):
    return lax.dot_general(
        left_side, right_side, (((0,), (0,)), ((), ())), preferred_element_type=jnp.float32
    ).reshape(-1)


def weight_rows(flats):
    return (
        flats[0].reshape(-1, 3 * D).astype(jnp.bfloat16),
        flats[1].reshape(-1, D).astype(jnp.bfloat16),
        flats[2].reshape(-1, FF).astype(jnp.bfloat16),
        flats[3].reshape(-1, D).astype(jnp.bfloat16),
        flats[4].astype(jnp.bfloat16),
    )


def adam_step(param, grad, moment, square):
    moment_new = beta_first * moment + (1.0 - beta_first) * grad
    square_new = beta_second * square + (1.0 - beta_second) * grad * grad
    moment_hat = moment_new / (1.0 - beta_first**3)
    square_hat = square_new / (1.0 - beta_second**3)
    change = -learn_rate * (moment_hat / (jnp.sqrt(square_hat) + adam_eps) + weight_decay * param)
    updated = param + change
    return (updated, moment_new, square_new, change)


def forward_pass(inputs, live_mask, matrices):
    qkv_matrix, proj_matrix, up_matrix, down_matrix, vector_values = matrices
    (
        gain_one,
        bias_one,
        bias_query,
        bias_value,
        bias_proj,
        gain_two,
        bias_two,
        bias_up,
        bias_down,
    ) = split_vectors(vector_values)
    slot_count = inputs.shape[0]
    seq_len = inputs.shape[1]
    row_count = slot_count * seq_len
    head_shape = (slot_count, seq_len, HEADS, HD)
    score_scale = 1.0 / math.sqrt(HD)
    flat_rows = inputs.reshape(row_count, D)
    normed_one, inverse_one = norm_stats(flat_rows)
    act_one = (normed_one * gain_one + bias_one).astype(jnp.bfloat16)
    projected = mixed_dot(act_one, qkv_matrix)
    query_rows = (projected[:, :D] + bias_query).astype(jnp.bfloat16).reshape(head_shape)
    key_rows = projected[:, D : 2 * D].astype(jnp.bfloat16).reshape(head_shape)
    value_rows = (projected[:, 2 * D :] + bias_value).astype(jnp.bfloat16).reshape(head_shape)
    scores = low_einsum("sqhe,skhe->shqk", query_rows, key_rows) * score_scale
    row_max = jnp.max(scores, axis=-1, keepdims=True)
    log_total = row_max + jnp.log(jnp.sum(jnp.exp(scores - row_max), axis=-1, keepdims=True))
    probs_low = jnp.exp(scores - log_total).astype(jnp.bfloat16)
    mixed_heads = (
        low_einsum("shqk,skhe->sqhe", probs_low, value_rows)
        .astype(jnp.bfloat16)
        .reshape(row_count, D)
    )
    hidden = flat_rows + mixed_dot(mixed_heads, proj_matrix) + bias_proj
    normed_two, inverse_two = norm_stats(hidden)
    act_two = (normed_two * gain_two + bias_two).astype(jnp.bfloat16)
    pre_act = mixed_dot(act_two, up_matrix) + bias_up
    gelu_value, gelu_slope = gelu_parts(pre_act)
    gelu_low = gelu_value.astype(jnp.bfloat16)
    block_rows = hidden + mixed_dot(gelu_low, down_matrix) + bias_down
    block_out = block_rows.reshape(inputs.shape) * live_mask
    saved = (
        normed_one,
        inverse_one,
        act_one,
        query_rows,
        key_rows,
        value_rows,
        log_total,
        mixed_heads,
        normed_two,
        inverse_two,
        act_two,
        gelu_low,
        gelu_slope,
    )
    return (block_out, saved)


def mlp_backward(saved, grad_rows, matrices):
    normed_two, inverse_two, gelu_slope = (saved[8], saved[9], saved[12])
    up_matrix, down_matrix, vector_values = (matrices[2], matrices[3], matrices[4])
    gain_two = split_vectors(vector_values)[5]
    grad_low = grad_rows.astype(jnp.bfloat16)
    grad_pre = mixed_dot(grad_low, down_matrix.T) * gelu_slope
    grad_pre_low = grad_pre.astype(jnp.bfloat16)
    grad_act_two = mixed_dot(grad_pre_low, up_matrix.T)
    grad_hidden = grad_rows + norm_back(grad_act_two * gain_two, normed_two, inverse_two)
    mlp_sums = [
        jnp.sum(grad_act_two * normed_two, axis=0),
        jnp.sum(grad_act_two, axis=0),
        jnp.sum(grad_pre, axis=0),
        jnp.sum(grad_rows, axis=0),
    ]
    return (grad_hidden, grad_low, grad_pre_low, mlp_sums)


def attn_backward(saved, grad_hidden, matrices):
    normed_one, inverse_one, query_rows, key_rows, value_rows, log_total = (
        saved[0],
        saved[1],
        saved[3],
        saved[4],
        saved[5],
        saved[6],
    )
    qkv_matrix, proj_matrix, vector_values = (matrices[0], matrices[1], matrices[4])
    gain_one = split_vectors(vector_values)[0]
    head_shape = query_rows.shape
    row_count = head_shape[0] * head_shape[1]
    score_scale = 1.0 / math.sqrt(HD)
    grad_hidden_low = grad_hidden.astype(jnp.bfloat16)
    grad_mixed = mixed_dot(grad_hidden_low, proj_matrix.T).astype(jnp.bfloat16).reshape(head_shape)
    scores = low_einsum("sqhe,skhe->shqk", query_rows, key_rows) * score_scale
    attn_probs = jnp.exp(scores - log_total)
    probs_low = attn_probs.astype(jnp.bfloat16)
    grad_probs = low_einsum("sqhe,skhe->shqk", grad_mixed, value_rows)
    grad_value = low_einsum("shqk,sqhe->skhe", probs_low, grad_mixed).reshape(row_count, D)
    row_delta = jnp.sum(attn_probs * grad_probs, axis=-1, keepdims=True)
    grad_scores = (attn_probs * (grad_probs - row_delta) * score_scale).astype(jnp.bfloat16)
    grad_query = low_einsum("shqk,skhe->sqhe", grad_scores, key_rows).reshape(row_count, D)
    grad_key = low_einsum("shqk,sqhe->skhe", grad_scores, query_rows).reshape(row_count, D)
    grad_proj_low = jnp.concatenate([grad_query, grad_key, grad_value], axis=1).astype(jnp.bfloat16)
    grad_act_one = mixed_dot(grad_proj_low, qkv_matrix.T)
    input_rows = grad_hidden + norm_back(grad_act_one * gain_one, normed_one, inverse_one)
    attn_sums = [
        jnp.sum(grad_act_one * normed_one, axis=0),
        jnp.sum(grad_act_one, axis=0),
        jnp.sum(grad_query, axis=0),
        jnp.sum(grad_value, axis=0),
        jnp.sum(grad_hidden, axis=0),
    ]
    return (input_rows, grad_proj_low, grad_hidden_low, attn_sums)


def body(
    inputs,
    cotangent,
    counts,
    qkv_weight,
    proj_weight,
    up_weight,
    down_weight,
    vectors,
    qkv_moment,
    proj_moment,
    up_moment,
    down_moment,
    vectors_moment,
    qkv_square,
    proj_square,
    up_square,
    down_square,
    vectors_square,
):
    shards = (qkv_weight, proj_weight, up_weight, down_weight, vectors)
    gathered = lax.all_gather(as_sent(weight_rows(shards)), ("dp", "fsdp"), axis=0, tiled=True)
    matrices = gathered[:4] + (gathered[4].astype(jnp.float32),)
    slot_count = inputs.shape[0]
    live_mask = (
        (jnp.arange(slot_count, dtype=jnp.int32) < counts[0])
        .astype(jnp.float32)
        .reshape(slot_count, 1, 1)
    )
    block_out, saved = forward_pass(inputs, live_mask, matrices)
    act_one, mixed_heads, act_two, gelu_low = (saved[2], saved[7], saved[10], saved[11])
    grad_rows = (cotangent * live_mask).reshape(-1, D)
    grad_hidden, grad_low, grad_pre_low, mlp_sums = mlp_backward(saved, grad_rows, matrices)
    down_full = outer_sum(gelu_low, grad_low)
    up_full = outer_sum(act_two, grad_pre_low)
    input_rows, grad_proj_low, grad_hidden_low, attn_sums = attn_backward(
        saved, grad_hidden, matrices
    )
    vectors_grad = jnp.concatenate(attn_sums + mlp_sums)
    qkv_full = outer_sum(act_one, grad_proj_low)
    proj_full = outer_sum(mixed_heads, grad_hidden_low)
    qkv_total, proj_total, up_total, down_total, vectors_total = (
        lax.psum_scatter(qkv_full, ("dp", "fsdp"), scatter_dimension=0, tiled=True),
        lax.psum_scatter(proj_full, ("dp", "fsdp"), scatter_dimension=0, tiled=True),
        lax.psum_scatter(up_full, ("dp", "fsdp"), scatter_dimension=0, tiled=True),
        lax.psum_scatter(down_full, ("dp", "fsdp"), scatter_dimension=0, tiled=True),
        lax.psum_scatter(vectors_grad, ("dp", "fsdp"), scatter_dimension=0, tiled=True),
    )
    input_grad = input_rows.reshape(inputs.shape)
    qkv_new = adam_step(qkv_weight, qkv_total, qkv_moment, qkv_square)
    proj_new = adam_step(proj_weight, proj_total, proj_moment, proj_square)
    up_new = adam_step(up_weight, up_total, up_moment, up_square)
    down_new = adam_step(down_weight, down_total, down_moment, down_square)
    vectors_new = adam_step(vectors, vectors_total, vectors_moment, vectors_square)
    return (
        block_out,
        input_grad,
        qkv_total,
        proj_total,
        up_total,
        down_total,
        vectors_total,
        qkv_new[0],
        proj_new[0],
        up_new[0],
        down_new[0],
        vectors_new[3],
        qkv_new[1],
        proj_new[1],
        up_new[1],
        down_new[1],
        vectors_new[1],
        qkv_new[2],
        proj_new[2],
        up_new[2],
        down_new[2],
        vectors_new[2],
    )


def solution(mesh):
    placed = (
        P(("dp", "fsdp"), None, None),
        P(("dp", "fsdp"), None, None),
        P(("dp", "fsdp")),
        P(("dp", "fsdp")),
        P(("dp", "fsdp")),
        P(("dp", "fsdp")),
        P(("dp", "fsdp")),
        P(("dp", "fsdp")),
        P(("dp", "fsdp")),
        P(("dp", "fsdp")),
        P(("dp", "fsdp")),
        P(("dp", "fsdp")),
        P(("dp", "fsdp")),
        P(("dp", "fsdp")),
        P(("dp", "fsdp")),
        P(("dp", "fsdp")),
        P(("dp", "fsdp")),
        P(("dp", "fsdp")),
    )
    return jax.shard_map(
        body,
        mesh=mesh,
        in_specs=placed,
        out_specs=(
            P(("dp", "fsdp"), None, None),
            P(("dp", "fsdp"), None, None),
            P(("dp", "fsdp")),
            P(("dp", "fsdp")),
            P(("dp", "fsdp")),
            P(("dp", "fsdp")),
            P(("dp", "fsdp")),
            P(("dp", "fsdp")),
            P(("dp", "fsdp")),
            P(("dp", "fsdp")),
            P(("dp", "fsdp")),
            P(("dp", "fsdp")),
            P(("dp", "fsdp")),
            P(("dp", "fsdp")),
            P(("dp", "fsdp")),
            P(("dp", "fsdp")),
            P(("dp", "fsdp")),
            P(("dp", "fsdp")),
            P(("dp", "fsdp")),
            P(("dp", "fsdp")),
            P(("dp", "fsdp")),
            P(("dp", "fsdp")),
        ),
        check_vma=False,
    )
```

profile of v0, /device:TPU:0, one launch (start us, length us, event | category | flops | bytes accessed | tf_op | source)
XLA Modules:
  0.0 784.4 jit_solution(10917424250861029345)
XLA Ops:
  7.3 1.0 convert_element_type.81
  8.3 0.8 convert_element_type.82
  9.1 0.9 convert_element_type.89
  10.0 0.7 convert_element_type.90
  10.8 1.0 convert_element_type.92
  11.8 0.7 convert_element_type.93
  12.5 0.0 all-gather.11.cloned.1.call-start
  12.6 1.0 convert_element_type.95
  13.5 0.8 convert_element_type.96
  14.4 0.0 all-reduce.9.cloned.1.call-start
  15.1 0.3 dynamic-update-slice
  15.4 42.2 %all-reduce = bf16[9216]{0:T(1024)(128)(2,1)S(1)} all-reduce(bf16[9216]{0:T(1024)(128)(2,1)S(1)} %dynamic-update-slice), channel_id=1, replica_groups=mesh['dp'=4,'fsdp'=8] {'dp','fsdp'}, use_global_device_ids=true, to_apply=%add | all-reduce | flops 9216 | bytes 36864
  57.6 1.0 reduce_sum.175
  58.6 0.2 multiply_reduce_fusion.7
  58.9 15.9 %all-gather.5.cloned.1.call-done = bf16[768,2304]{1,0:T(8,128)(2,1)} async-done(((bf16[24,2304]{1,0:T(8,128)(2,1)}), bf16[768,2304]{1,0:T(8,128)(2,1)}) %all-gather.5.cloned.1.call-update) | async-done | bytes 3538960 | tf_op jit(solution)/shard_map/all_gather | solution.py:229
  74.8 3.0 fusion.45
  77.8 0.1 fusion.27
  77.9 0.9 copy.67
  78.8 0.2 copy.68
  79.0 0.9 copy.66
  79.9 1.6 multiply_reduce_fusion.1
  81.5 0.5 exponential_reduce_fusion
  82.0 0.6 convolution_convert_fusion
  82.6 48.7 %all-gather.7.cloned.1.call-done = bf16[768,768]{1,0:T(8,128)(2,1)} async-done(((bf16[24,768]{1,0:T(8,128)(2,1)}), bf16[768,768]{1,0:T(8,128)(2,1)}) %all-gather.7.cloned.1.call-update) | async-done | bytes 1179664 | tf_op jit(solution)/shard_map/all_gather | solution.py:229
  131.4 1.8 fusion.69
  133.2 0.8 copy-done.1
  134.0 0.2 multiply_reduce_fusion.6
  134.2 63.4 %all-gather.9.cloned.1.call-done = bf16[768,3072]{1,0:T(8,128)(2,1)} async-done(((bf16[24,3072]{1,0:T(8,128)(2,1)}), bf16[768,3072]{1,0:T(8,128)(2,1)}) %all-gather.9.cloned.1.call-update) | async-done | bytes 4718608 | tf_op jit(solution)/shard_map/all_gather | solution.py:229
  197.7 5.2 convolution_add_fusion
  202.8 60.8 %all-gather.11.cloned.1.call-done = bf16[3072,768]{1,0:T(8,128)(2,1)} async-done(((bf16[96,768]{1,0:T(8,128)(2,1)}), bf16[3072,768]{1,0:T(8,128)(2,1)}) %all-gather.11.cloned.1.call-update) | async-done | bytes 4718608 | tf_op jit(solution)/shard_map/all_gather | solution.py:229
  263.6 5.2 fusion.72
  268.9 1.9 multiply_reduce_fusion.2
  270.8 0.3 fusion.65
  271.1 0.8 copy-done.5
  271.9 0.2 copy-done.10
  272.1 1.3 convolution_convert_fusion.1
  273.4 1.9 copy.71
  275.3 2.4 fusion.66
  277.7 2.0 fusion.73
  279.7 4.5 fusion.18
  284.2 4.7 fusion.67
  288.9 3.1 fusion.41
  292.0 4.6 fusion.44
  296.6 5.3 convolution_bitcast_fusion
  302.0 3.3 reshape.238
  305.3 4.2 fusion.33
  309.5 7.9 %reshape.237 = f32[1769472]{0:T(1024)} reshape(f32[768,2304]{1,0:T(8,128)} %fusion.33) | data formatting | bytes 14155776 | tf_op jit(solution)/shard_map/reshape | solution.py:69
  317.5 10.8 %reshape.240 = f32[2359296]{0:T(1024)} reshape(f32[3072,768]{1,0:T(8,128)} %fusion.44) | data formatting | bytes 18874368 | tf_op jit(solution)/shard_map/reshape | solution.py:69
  328.3 9.6 %copy.82 = f32[96,24,8,128]{3,1,2,0:T(8,128)} copy(f32[96,24,8,128]{3,2,1,0:T(8,128)} %convolution_bitcast_fusion) | data formatting | bytes 18874368
  337.9 0.1 fusion.35
  338.0 4.4 fusion.25
  342.4 1.4 copy.75
  343.8 0.1 reduce_sum.190
  343.9 0.1 reduce_sum.188
  344.0 3.6 multiply_reduce_fusion.3
  347.7 0.2 add_bitcast_fusion
  347.9 1.4 copy.76
  349.5 41.9 %all-reduce.5 = f32[9216]{0:T(1024)S(1)} all-reduce(f32[9216]{0:T(1024)S(1)} %constant_dynamic-update-slice_fusion), channel_id=6, replica_groups=mesh['dp'=4,'fsdp'=8] {'dp','fsdp'}, use_global_device_ids=true, to_apply=%region_24.0.clone | all-reduce | flops 9216 | bytes 73728
  391.4 0.7 add_multiply_fusion.1
  392.1 378.1 %all-reduce.9.cloned.1.call-done = (f32[1769472]{0:T(1024)}, f32[589824]{0:T(1024)}, f32[2359296]{0:T(1024)}, f32[2359296]{0:T(1024)}) async-done(((f32[1769472]{0:T(1024)}, f32[589824]{0:T(1024)}, f32[2359296]{0:T(1024)}, f32[2359296]{0:T(1024)}), (f32[1769472]{0:T(1024)}, f32[589824]{0:T(1024)}, f32[2359296]{0:T(1024)}, f32[2359296]{0:T(1024)})) %all-reduce.9.cloned.1.call-update) | async-done | bytes 28311568
  770.2 2.0 multiply_add_fusion.2
  772.3 2.1 multiply_add_fusion
  774.4 1.9 multiply_add_fusion.4
  776.3 1.6 multiply_add_fusion.6
  (98 shorter events, 0.5 us)
Async XLA Ops:
  7.2 7.9 %copy-start.32 = (f32[288]{0:T(512)S(1)}, f32[288]{0:T(512)}, u32[]{:S(2)}) copy-start(f32[288]{0:T(512)} %param.25) | copy-start | bytes 3460
  7.2 50.4 %copy-start = (f32[1,197,768]{2,0,1:T(1,128)S(1)}, f32[1,197,768]{2,0,1:T(1,128)}, u32[]{:S(2)}) copy-start(f32[1,197,768]{2,0,1:T(1,128)} %param.18) | copy-start | bytes 1815556
  7.2 67.6 %all-gather.5.cloned.1.call-start = ((), (), s32[]{:S(2)}) async-start(), calls=%async_computation | async-start | bytes 3649536 | tf_op jit(solution)/shard_map/all_gather | solution.py:229
  9.1 122.3 %all-gather.7.cloned.1.call-start = ((), (), s32[]{:S(2)}) async-start(), calls=%async_computation.1 | async-start | bytes 1216512 | tf_op jit(solution)/shard_map/all_gather | solution.py:229
  10.7 186.9 %all-gather.9.cloned.1.call-start = ((), (), s32[]{:S(2)}) async-start(), calls=%async_computation.2 | async-start | bytes 4866048 | tf_op jit(solution)/shard_map/all_gather | solution.py:229
  12.5 251.1 %all-gather.11.cloned.1.call-start = ((), (), s32[]{:S(2)}) async-start(), calls=%async_computation.3 | async-start | bytes 4866048 | tf_op jit(solution)/shard_map/all_gather | solution.py:229
  14.4 755.8 %all-reduce.9.cloned.1.call-start = ((), (), s32[]{:S(2)}) async-start(), calls=%async_computation.4 | async-start | bytes 56623104
  79.0 3.0 copy-start.15
  79.9 2.1 copy-start.11
  133.2 0.8 copy-start.1
  263.6 5.2 copy-start.2
  263.6 5.2 copy-start.9
  268.8 1.9 copy-start.16
  268.8 1.9 copy-start.7
  270.7 1.3 copy-start.10
  271.1 0.8 copy-start.5
  275.3 2.4 copy-start.12
  275.3 2.4 copy-start.13
  288.9 3.1 copy-start.4
  288.9 3.1 copy-start.8
  292.0 4.6 copy-start.3
  292.0 4.6 copy-start.17
  302.0 3.3 copy-start.14
  302.0 3.3 copy-start.21
  302.0 3.3 copy-start.22
  344.0 3.7 copy-start.6
  347.6 43.9 %copy-start.33 = (f32[288]{0:T(512)S(1)}, f32[288]{0:T(512)}, u32[]{:S(2)}) copy-start(f32[288]{0:T(512)} %param.30) | copy-start | bytes 3460
  347.6 43.9 %copy-start.34 = (f32[288]{0:T(512)S(1)}, f32[288]{0:T(512)}, u32[]{:S(2)}) copy-start(f32[288]{0:T(512)} %param.35) | copy-start | bytes 3460
  347.6 422.6 %copy-start.18 = (f32[73728]{0:T(1024)S(1)}, f32[73728]{0:T(1024)}, u32[]{:S(2)}) copy-start(f32[73728]{0:T(1024)} %param.23) | copy-start | bytes 884740
  347.6 422.6 %copy-start.23 = (f32[73728]{0:T(1024)S(1)}, f32[73728]{0:T(1024)}, u32[]{:S(2)}) copy-start(f32[73728]{0:T(1024)} %param.28) | copy-start | bytes 884740
  347.6 422.6 %copy-start.24 = (f32[73728]{0:T(1024)S(1)}, f32[73728]{0:T(1024)}, u32[]{:S(2)}) copy-start(f32[73728]{0:T(1024)} %param.33) | copy-start | bytes 884740
  347.9 424.3 %copy-start.19 = (f32[73728]{0:T(1024)S(1)}, f32[73728]{0:T(1024)}, u32[]{:S(2)}) copy-start(f32[73728]{0:T(1024)} %param.24) | copy-start | bytes 884740
  347.9 424.3 %copy-start.25 = (f32[73728]{0:T(1024)S(1)}, f32[73728]{0:T(1024)}, u32[]{:S(2)}) copy-start(f32[73728]{0:T(1024)} %param.29) | copy-start | bytes 884740
  347.9 424.3 %copy-start.26 = (f32[73728]{0:T(1024)S(1)}, f32[73728]{0:T(1024)}, u32[]{:S(2)}) copy-start(f32[73728]{0:T(1024)} %param.34) | copy-start | bytes 884740
  349.4 425.0 %copy-start.20 = (f32[55296]{0:T(1024)S(1)}, f32[55296]{0:T(1024)}, u32[]{:S(2)}) copy-start(f32[55296]{0:T(1024)} %param.21) | copy-start | bytes 663556
  349.4 425.0 %copy-start.28 = (f32[55296]{0:T(1024)S(1)}, f32[55296]{0:T(1024)}, u32[]{:S(2)}) copy-start(f32[55296]{0:T(1024)} %param.26) | copy-start | bytes 663556
  349.4 425.0 %copy-start.29 = (f32[55296]{0:T(1024)S(1)}, f32[55296]{0:T(1024)}, u32[]{:S(2)}) copy-start(f32[55296]{0:T(1024)} %param.31) | copy-start | bytes 663556
  772.2 4.0 copy-start.27
  772.2 4.0 copy-start.30
  772.2 4.0 copy-start.31
Sparse Core Ops, SparseCore 0:
  11.6 63.0 all-gather.4
  78.4 52.9 all-gather.6
  135.0 62.6 all-gather.8
  201.1 62.4 all-gather.10
  338.0 432.1 all-reduce.8
where the time goes:
time: 786 us; the launch traced here: 784 us
  waiting for transfers between devices  567 us (72%)
  blocking collectives  84.1 us (11%)
  matrix products  59.4 us (8%)
  local copies, waits for them, and re-layouts  43.9 us (6%)
  between operations  15 us (2%)
  other arithmetic  14.8 us (2%)
    unnamed x6, waiting for transfers between devices  378 us
    all_gather x4, waiting for transfers between devices, body(): lax.all_gather(as_sent(weight_rows(shards)), ('dp', 'fsdp'), axis=0, tile...  189 us
    unnamed x2, blocking collectives  84.1 us
    dot_general x8, matrix products, mixed_dot(): return jnp.dot(left_side, right_side, preferred_element_type=jnp.float32)  26.3 us
    reshape x3, local copies, waits for them, and re-layouts, outer_sum(): return lax.dot_general(left_side, right_side, (((0,), (0,)), ((), ())), p...  22 us
    dot_general x4, matrix products, outer_sum(): lax.dot_general(left_side, right_side, (((0,), (0,)), ((), ())), preferre...  17.3 us
    dot_general x6, matrix products, low_einsum(): jnp.einsum(form, left_side, right_side, preferred_element_type=jnp.float32)  15.8 us
  transfers between devices with their start and end apart: 5, of which 5 were waited for; matrix products, arithmetic and copies ran while one was open for 4% of the time, Pallas kernels for 0%

commit v1 on v0

--- a/solution.py
+++ b/solution.py
@@ -1,8 +1,11 @@
+import functools
 import math
 
 import jax
 import jax.numpy as jnp
 from jax import lax
+from jax.experimental import pallas as pl
+from jax.experimental.pallas import tpu as pltpu
 from jax.sharding import PartitionSpec as P
 
 D = 768
@@ -17,14 +20,6 @@
 adam_eps = 1e-08
 learn_rate = 0.02
 weight_decay = 0.05
-
-
-def as_sent(shard):
-
-    def short(part):
-        return part.astype(jnp.bfloat16) if part.dtype == jnp.float32 else part
-
-    return jax.tree.map(short, shard)
 
 
 def norm_stats(values):
@@ -66,17 +61,331 @@
 def outer_sum(left_side, right_side):
     return lax.dot_general(
         left_side, right_side, (((0,), (0,)), ((), ())), preferred_element_type=jnp.float32
-    ).reshape(-1)
-
-
-def weight_rows(flats):
+    )
+
+
+def block_rows_of(per):
+    rows = -(-(12 * per + 1) // 8) * 8
+    return rows if rows % 16 else rows + 8
+
+
+def pack_shards(per, shards):
+    qkv, proj, up, down, vectors = (shard.astype(jnp.bfloat16) for shard in shards)
+    vec_row = jnp.pad(vectors, (0, D - vectors.shape[0])).reshape(1, D)
+    parts = [qkv.reshape(per, 3 * D)[:, k * D : (k + 1) * D] for k in range(3)]
+    parts.append(proj.reshape(per, D))
+    parts += [up.reshape(per, FF)[:, k * D : (k + 1) * D] for k in range(4)]
+    tail = block_rows_of(per) - 12 * per
+    parts += [down.reshape(4 * per, D), jnp.pad(vec_row, ((0, tail - 1), (0, 0)))]
+    return jnp.concatenate(parts, axis=0)
+
+
+def unpack_matrices(per, blocks, vec_part):
+    def piece(at):
+        return blocks[:, at * per : (at + 1) * per].reshape(D, D)
+
+    qkv_matrix = jnp.concatenate([piece(k) for k in range(3)], axis=1)
+    up_matrix = jnp.concatenate([piece(4 + k) for k in range(4)], axis=1)
+    down_matrix = blocks[:, 8 * per : 12 * per].reshape(FF, D)
+    vector_values = blocks[:, 12 * per, :vec_part].reshape(-1).astype(jnp.float32)
+    return (qkv_matrix, piece(3), up_matrix, down_matrix, vector_values)
+
+
+def pack_grads(per, total, grads):
+    low = [grad.astype(jnp.bfloat16) for grad in grads]
+    vec_part = grads[4].shape[0] // total
+    vec_cols = -(-vec_part // 128) * 128
+    vec = jnp.pad(low[4].reshape(total, 1, vec_part), ((0, 0), (0, 15), (0, vec_cols - vec_part)))
+    if per % 8 == 0:
+        return [grad.reshape(total, -1, grad.shape[1]) for grad in low[:4]] + [vec]
+
+    def piece(full, k):
+        return full[:, k * D : (k + 1) * D].reshape(total, per, D)
+
+    parts = [piece(low[0], k) for k in range(3)] + [piece(low[1], 0)]
+    parts += [piece(low[2], k) for k in range(4)] + [low[3].reshape(total, 4 * per, D)]
+    tail = block_rows_of(per) - 12 * per
+    parts.append(jnp.pad(vec[:, :1], ((0, 0), (0, tail - 1), (0, D - vec_cols))))
+    return [jnp.concatenate(parts, axis=1)]
+
+
+def unpack_grads(per, pieces, vec_part):
+    if len(pieces) > 1:
+        return [piece.reshape(-1) for piece in pieces[:4]] + [pieces[4][0, :vec_part]]
+    block = pieces[0]
+
+    def side(first, count):
+        return jnp.concatenate(
+            [block[(first + k) * per : (first + k + 1) * per] for k in range(count)], axis=1
+        ).reshape(-1)
+
     return (
-        flats[0].reshape(-1, 3 * D).astype(jnp.bfloat16),
-        flats[1].reshape(-1, D).astype(jnp.bfloat16),
-        flats[2].reshape(-1, FF).astype(jnp.bfloat16),
-        flats[3].reshape(-1, D).astype(jnp.bfloat16),
-        flats[4].astype(jnp.bfloat16),
-    )
+        side(0, 3),
+        block[3 * per : 4 * per].reshape(-1),
+        side(4, 4),
+        block[8 * per : 12 * per].reshape(-1),
+        block[12 * per, :vec_part],
+    )
+
+
+def remote(src, dst, send, recv, where):
+    return pltpu.make_async_remote_copy(
+        src_ref=src, dst_ref=dst, send_sem=send, recv_sem=recv,
+        device_id=where, device_id_type=pl.DeviceIdType.MESH,
+    )
+
+
+def greet_all(pair, dp_peer, z_peer, ndp, nz):
+    barrier = pltpu.get_barrier_semaphore()
+
+    def greet(where):
+        pl.semaphore_signal(barrier, inc=1, device_id=where, device_id_type=pl.DeviceIdType.MESH)
+
+    greet(pair)
+    for j in range(1, ndp):
+        greet(dp_peer(j))
+    lax.fori_loop(1, nz, lambda j, carry: (greet(z_peer(j)), carry)[1], 0)
+    pl.semaphore_wait(barrier, 1 + (ndp - 1) + (nz - 1))
+
+
+def gather_kernel(ndp, nz, in_ref, out_ref, own_sem, zs, zr, ds, dr, ps, pr):
+    d, f = lax.axis_index("dp"), lax.axis_index("fsdp")
+    z, c = f // 2, f % 2
+    pair = (d, z * 2 + 1 - c)
+
+    def dp_peer(j):
+        return (lax.rem(d + j, ndp), f)
+
+    def z_peer(j):
+        return (d, lax.rem(z + j, nz) * 2 + c)
+
+    greet_all(pair, dp_peer, z_peer, ndp, nz)
+
+    def from_z(t):
+        return lax.rem(z - t + nz, nz)
+
+    def from_dp(j):
+        return lax.rem(d - j + ndp, ndp)
+
+    def place(i, t, core):
+        return out_ref.at[i, from_z(t), core]
+
+    def z_send(t):
+        return remote(in_ref, out_ref.at[d, z, c], zs.at[t - 1], zr.at[t - 1], z_peer(t))
+
+    def z_arrival(t):
+        return remote(in_ref, place(d, t, c), zs.at[t - 1], zr.at[t - 1], z_peer(t))
+
+    def dp_send(t, j):
+        return remote(
+            place(d, t, c), place(d, t, c), ds.at[t, j - 1], dr.at[t, j - 1], dp_peer(j)
+        )
+
+    def dp_arrival(t, j):
+        there = place(from_dp(j), t, c)
+        return remote(there, there, ds.at[t, j - 1], dr.at[t, j - 1], dp_peer(j))
+
+    def pair_send(t, j):
+        here = place(from_dp(j), t, c)
+        return remote(here, here, ps.at[t, j], pr.at[t, j], pair)
+
+    def pair_arrival(t, j):
+        there = place(from_dp(j), t, 1 - c)
+        return remote(there, there, ps.at[t, j], pr.at[t, j], pair)
+
+    lax.fori_loop(1, nz, lambda t, carry: (z_send(t).start(), carry)[1], 0)
+    own = pltpu.make_async_copy(in_ref, out_ref.at[d, z, c], own_sem)
+    own.start()
+    own.wait()
+
+    def forward(t):
+        for j in range(1, ndp):
+            dp_send(t, j).start()
+        pair_send(t, 0).start()
+
+    def spread(t):
+        for j in range(1, ndp):
+            dp_arrival(t, j).wait_recv()
+            pair_send(t, j).start()
+
+    def middle(t, carry):
+        z_arrival(t).wait_recv()
+        forward(t)
+        spread(t - 1)
+        return carry
+
+    forward(0)
+    lax.fori_loop(1, nz, middle, 0)
+    spread(nz - 1)
+
+    def close(t, carry):
+        for j in range(ndp):
+            pair_arrival(t, j).wait_recv()
+            pair_send(t, j).wait_send()
+        for j in range(1, ndp):
+            dp_send(t, j).wait_send()
+        return carry
+
+    lax.fori_loop(0, nz, close, 0)
+    lax.fori_loop(1, nz, lambda t, carry: (z_send(t).wait_send(), carry)[1], 0)
+
+
+def gather_blocks(block, ndp, nf):
+    rows = block.shape[0]
+    nz = nf // 2
+    dma = pltpu.SemaphoreType.DMA
+    gathered = pl.pallas_call(
+        functools.partial(gather_kernel, ndp, nz),
+        out_shape=jax.ShapeDtypeStruct((ndp, nz, 2, rows, D), jnp.bfloat16),
+        in_specs=[pl.BlockSpec(memory_space=pltpu.VMEM)],
+        out_specs=pl.BlockSpec(memory_space=pl.ANY),
+        scratch_shapes=[
+            dma(()),
+            dma((nz - 1,)),
+            dma((nz - 1,)),
+            dma((nz, ndp - 1)),
+            dma((nz, ndp - 1)),
+            dma((nz, ndp)),
+            dma((nz, ndp)),
+        ],
+        compiler_params=pltpu.CompilerParams(
+            collective_id=1, has_side_effects=True, vmem_limit_bytes=16 * 1024 * 1024
+        ),
+    )(block)
+    return gathered.reshape(ndp * nf, rows, D)
+
+
+def scatter_kernel(ndp, nz, count, *refs):
+    g_refs, out_refs, pair_bufs, dp_bufs, z_bufs = (
+        refs[k * count : (k + 1) * count] for k in range(5)
+    )
+    ps, pr, ds, dr, zs, zr = refs[5 * count :]
+    pieces = range(count)
+    d, f = lax.axis_index("dp"), lax.axis_index("fsdp")
+    z, c = f // 2, f % 2
+    oc = 1 - c
+    pair = (d, z * 2 + oc)
+    wide = jnp.float32
+
+    def dp_peer(j):
+        return (lax.rem(d + j, ndp), f)
+
+    def z_peer(j):
+        return (d, lax.rem(z + j, nz) * 2 + c)
+
+    greet_all(pair, dp_peer, z_peer, ndp, nz)
+
+    def target_z(t):
+        return lax.rem(z + t + 1, nz)
+
+    def pair_copy(t, i, k):
+        return remote(
+            g_refs[k].at[i, target_z(t), oc], pair_bufs[k].at[t, i],
+            ps.at[t, i, k], pr.at[t, i, k], pair,
+        )
+
+    def dp_copy(t, j, k):
+        where = dp_peer(j)
+        return remote(
+            pair_bufs[k].at[t, where[0]], dp_bufs[k].at[t, j - 1],
+            ds.at[t, j - 1, k], dr.at[t, j - 1, k], where,
+        )
+
+    def z_copy(t, k):
+        return remote(
+            dp_bufs[k].at[t, 0], z_bufs[k].at[t], zs.at[t, k], zr.at[t, k], z_peer(t + 1)
+        )
+
+    def dp_of(j):
+        return lax.rem(d + j, ndp)
+
+    def open_pair(t):
+        for j in range(1, ndp + 1):
+            for k in pieces:
+                pair_copy(t, dp_of(j), k).start()
+
+    def chip_sum(t):
+        for j in range(1, ndp + 1):
+            i = dp_of(j)
+            for k in pieces:
+                pair_copy(t, i, k).wait_recv()
+                mine = g_refs[k][i, target_z(t), c].astype(wide)
+                pair_bufs[k][t, i] = (pair_bufs[k][t, i].astype(wide) + mine).astype(jnp.bfloat16)
+                if j < ndp:
+                    dp_copy(t, j, k).start()
+
+    def dp_sum(t, k):
+        running = pair_bufs[k][t, d].astype(wide)
+        for j in range(1, ndp):
+            dp_copy(t, j, k).wait_recv()
+            running = running + dp_bufs[k][t, j - 1].astype(wide)
+        return running
+
+    def middle(t, carry):
+        chip_sum(t)
+        for k in pieces:
+            dp_bufs[k][t - 1, 0] = dp_sum(t - 1, k).astype(jnp.bfloat16)
+            z_copy(t - 1, k).start()
+        return carry
+
+    lax.fori_loop(0, nz, lambda t, carry: (open_pair(t), carry)[1], 0)
+    chip_sum(0)
+    lax.fori_loop(1, nz, middle, 0)
+    for k in pieces:
+        out_refs[k][...] = dp_sum(nz - 1, k)
+
+    def last(t, carry):
+        for k in pieces:
+            z_copy(t, k).wait_recv()
+            out_refs[k][...] += z_bufs[k][t].astype(wide)
+        return carry
+
+    lax.fori_loop(0, nz - 1, last, 0)
+
+    def close(t, carry):
+        for k in pieces:
+            for i in range(ndp):
+                pair_copy(t, i, k).wait_send()
+            for j in range(1, ndp):
+                dp_copy(t, j, k).wait_send()
+        return carry
+
+    lax.fori_loop(0, nz, close, 0)
+
+    def close_z(t, carry):
+        for k in pieces:
+            z_copy(t, k).wait_send()
+        return carry
+
+    lax.fori_loop(0, nz - 1, close_z, 0)
+
+
+def scatter_sum(pieces, ndp, nf):
+    nz = nf // 2
+    count = len(pieces)
+    dma = pltpu.SemaphoreType.DMA
+    shapes = [piece.shape[1:] for piece in pieces]
+    whole_ref = pl.BlockSpec(memory_space=pltpu.VMEM)
+    return pl.pallas_call(
+        functools.partial(scatter_kernel, ndp, nz, count),
+        out_shape=[jax.ShapeDtypeStruct(shape, jnp.float32) for shape in shapes],
+        in_specs=[whole_ref] * count,
+        out_specs=[whole_ref] * count,
+        scratch_shapes=[pltpu.VMEM((nz, ndp) + shape, jnp.bfloat16) for shape in shapes]
+        + [pltpu.VMEM((nz, ndp - 1) + shape, jnp.bfloat16) for shape in shapes]
+        + [pltpu.VMEM((nz - 1,) + shape, jnp.bfloat16) for shape in shapes]
+        + [
+            dma((nz, ndp, count)),
+            dma((nz, ndp, count)),
+            dma((nz, ndp - 1, count)),
+            dma((nz, ndp - 1, count)),
+            dma((nz - 1, count)),
+            dma((nz - 1, count)),
+        ],
+        compiler_params=pltpu.CompilerParams(
+            collective_id=0, has_side_effects=True, vmem_limit_bytes=50 * 1024 * 1024
+        ),
+    )(*[piece.reshape((ndp, nz, 2) + shape) for piece, shape in zip(pieces, shapes)])
 
 
 def adam_step(param, grad, moment, square):
@@ -206,6 +515,8 @@
 
 
 def body(
+    ndp,
+    nf,
     inputs,
     cotangent,
     counts,
@@ -226,8 +537,11 @@
     vectors_square,
 ):
     shards = (qkv_weight, proj_weight, up_weight, down_weight, vectors)
-    gathered = lax.all_gather(as_sent(weight_rows(shards)), ("dp", "fsdp"), axis=0, tiled=True)
-    matrices = gathered[:4] + (gathered[4].astype(jnp.float32),)
+    total = ndp * nf
+    per = D // total
+    vec_part = vectors.shape[0]
+    gathered = gather_blocks(pack_shards(per, shards), ndp, nf)
+    matrices = unpack_matrices(per, gathered, vec_part)
     slot_count = inputs.shape[0]
     live_mask = (
         (jnp.arange(slot_count, dtype=jnp.int32) < counts[0])
@@ -246,13 +560,9 @@
     vectors_grad = jnp.concatenate(attn_sums + mlp_sums)
     qkv_full = outer_sum(act_one, grad_proj_low)
     proj_full = outer_sum(mixed_heads, grad_hidden_low)
-    qkv_total, proj_total, up_total, down_total, vectors_total = (
-        lax.psum_scatter(qkv_full, ("dp", "fsdp"), scatter_dimension=0, tiled=True),
-        lax.psum_scatter(proj_full, ("dp", "fsdp"), scatter_dimension=0, tiled=True),
-        lax.psum_scatter(up_full, ("dp", "fsdp"), scatter_dimension=0, tiled=True),
-        lax.psum_scatter(down_full, ("dp", "fsdp"), scatter_dimension=0, tiled=True),
-        lax.psum_scatter(vectors_grad, ("dp", "fsdp"), scatter_dimension=0, tiled=True),
-    )
+    packed = pack_grads(per, total, (qkv_full, proj_full, up_full, down_full, vectors_grad))
+    summed = scatter_sum(packed, ndp, nf)
+    qkv_total, proj_total, up_total, down_total, vectors_total = unpack_grads(per, summed, vec_part)
     input_grad = input_rows.reshape(inputs.shape)
     qkv_new = adam_step(qkv_weight, qkv_total, qkv_moment, qkv_square)
     proj_new = adam_step(proj_weight, proj_total, proj_moment, proj_square)
@@ -307,7 +617,7 @@
         P(("dp", "fsdp")),
     )
     return jax.shard_map(
-        body,
+        functools.partial(body, mesh.shape["dp"], mesh.shape["fsdp"]),
         mesh=mesh,
         in_specs=placed,
         out_specs=(

time: 786 us -> 274 us (0.35)
  waiting for transfers between devices: 567 us -> 0 us
  Pallas kernels: 0 us -> 180 us
  blocking collectives: 84.1 us -> 0 us
  local copies, waits for them, and re-layouts: 43.9 us -> 29.4 us
  matrix products: 59.4 us -> 46.4 us
  between operations: 15 us -> 2.19 us
    unnamed x6 -> x0, waiting for transfers between devices: 378 us -> none
    all_gather x4 -> x0, waiting for transfers between devices: 189 us -> none  [body(): lax.all_gather(as_sent(weight_rows(shards)), ('dp', 'fsdp'), axis=0, tile...]
    pallas_call x0 -> x2, Pallas kernels: none -> 180 us  [the longest x1 91.9 us: scatter_sum(): pl.pallas_call(functools.partial(scatter_kernel, ndp, nz, count), out_sha...]
    unnamed x2 -> x0, blocking collectives: 84.1 us -> none
    reshape x3 -> x8, local copies, waits for them, and re-layouts: 22 us -> 0.47 us  [the longest x1 0.15 us: pack_shards(): parts = [qkv.reshape(per, 3 * D)[:, k * D:(k + 1) * D] for k in range(3)]]
    slice x1 -> x4, local copies, waits for them, and re-layouts: 0.01 us -> 11.9 us  [the longest x1 6.51 us: piece(): return blocks[:, at * per:(at + 1) * per].reshape(D, D)]
    dot_general x8, matrix products: 26.3 us -> 14.6 us  [mixed_dot(): return jnp.dot(left_side, right_side, preferred_element_type=jnp.float32)]
  transfers between devices with their start and end apart: 5 -> 0, of which waited for: 5 -> 0; matrix products, arithmetic and copies ran while one was open for 4% -> 0% of each run, Pallas kernels for 0% -> 0%
where the time goes in v1:
time: 274 us; the launch traced here: 273 us
  Pallas kernels  180 us (66%)
  matrix products  46.4 us (17%)
  local copies, waits for them, and re-layouts  29.4 us (11%)
  other arithmetic  15.3 us (6%)
    pallas_call x1, Pallas kernels, scatter_sum(): pl.pallas_call(functools.partial(scatter_kernel, ndp, nz, count), out_sha...  91.9 us
    pallas_call x1, Pallas kernels, gather_blocks(): pl.pallas_call(functools.partial(gather_kernel, ndp, nz), out_shape=jax.S...  87.9 us
    dot_general x6, matrix products, low_einsum(): jnp.einsum(form, left_side, right_side, preferred_element_type=jnp.float32)  18.4 us
    dot_general x8, matrix products, mixed_dot(): return jnp.dot(left_side, right_side, preferred_element_type=jnp.float32)  14.6 us
    dot_general x4, matrix products, outer_sum(): lax.dot_general(left_side, right_side, (((0,), (0,)), ((), ())), preferre...  13.4 us
    unnamed x132, local copies, waits for them, and re-layouts  13.1 us
    slice x1, local copies, waits for them, and re-layouts, piece(): return blocks[:, at * per:(at + 1) * per].reshape(D, D)  6.51 us

profile of v1, /device:TPU:0, one launch (start us, length us, event | category | flops | bytes accessed | tf_op | source)
XLA Modules:
  0.0 273.2 jit_solution(14519177846322736559)
XLA Ops:
  1.4 0.7 convert_element_type.107
  2.1 2.1 reduce_sum.175
  4.2 1.3 multiply_reduce_fusion.7
  5.5 1.1 fusion.35
  6.7 0.9 convert_element_type.104
  7.6 1.0 convert_element_type.103
  8.6 0.2 reshape.289
  8.9 0.1 reshape.292
  9.2 87.9 %shard_map.345 = bf16[4,4,2,296,768]{4,3,2,1,0:T(8,128)(2,1)S(1)} custom-call(bf16[296,768]{1,0:T(8,128)(2,1)S(1)} %constant_dynamic-update-slice_fusion.in_ref), custom_call_target="tpu_custom_call" | custom-call | tf_op jit(solution)/shard_map/pallas_call | solution.py:237
  97.1 5.2 %copy-done = bf16[4,4,2,296,768]{4,3,2,1,0:T(8,128)(2,1)} copy-done((bf16[4,4,2,296,768]{4,3,2,1,0:T(8,128)(2,1)}, bf16[4,4,2,296,768]{4,3,2,1,0:T(8,128)(2,1)S(1)}, u32[]{:S(2)}) %copy-start) | copy-done | bytes 14549016
  102.3 0.1 fusion.49
  102.5 0.6 fusion.75
  103.1 4.8 %slice.150 = bf16[32,96,768]{2,1,0:T(8,128)(2,1)} slice(bf16[32,296,768]{2,1,0:T(8,128)(2,1)} %bitcast.94), slice={[0:32], [192:288], [0:768]} | slice | bytes 9437184 | tf_op jit(solution)/shard_map/slice | solution.py:89
  107.9 6.5 %fusion.72 = (bf16[32,24,768]{2,1,0:T(8,128)(2,1)}, bf16[32,24,768]{2,1,0:T(8,128)(2,1)}, bf16[32,24,768]{2,1,0:T(8,128)(2,1)}, bf16[32,24,768]{2,1,0:T(8,128)(2...) fusion(bf16[32,296,768]{2,1,0:T(8,128)(2,1)} %bitcast.95), kind=kLoop, calls=%fused_computation.127 | loop fusion | bytes 18874368 | tf_op jit(solution)/shard_map/slice | solution.py:85
  114.5 1.0 fusion.15
  115.5 0.4 copy-done.20
  115.8 0.4 copy-done.21
  116.4 0.9 copy.56
  117.3 0.2 copy.57
  117.5 0.2 copy.55
  117.6 1.5 multiply_reduce_fusion.1
  119.2 0.5 exponential_reduce_fusion
  119.8 0.6 convolution_convert_fusion.4
  120.4 1.0 copy-done.2
  121.4 0.3 copy-done.6
  121.7 0.5 fusion.76
  122.2 0.2 multiply_reduce_fusion.6
  122.5 0.4 copy-done.22
  122.8 0.4 copy-done.23
  123.2 1.4 multiply_convert_fusion.1
  124.6 0.2 slice-done.1
  124.8 2.3 fusion.79
  127.1 1.2 fusion.27
  128.3 1.4 copy.65
  129.7 2.3 multiply_reduce_fusion.2
  132.1 0.3 fusion.71
  132.3 1.3 convolution_convert_fusion.5
  133.6 1.9 copy.60
  135.5 2.4 fusion.73
  138.0 1.7 convolution_convert_fusion.3
  139.7 2.0 fusion.80
  141.7 5.9 %fusion.20 = bf16[12,64,197]{2,1,0:T(8,128)(2,1)} fusion(bf16[197,12,64]{0,2,1:T(8,128)(2,1)S(1)} %bitcast.117, f32[12,197,197]{1,2,0:T(8,128)} %fusion.80, f32[12,197,197]{1,2,0:T(8,128)} %copy-done.1, f32[12,197]{1,0:T(8,128)S(1)} %log_add_fusion), kind=kOutput, calls=%fused_computation.30 | convolution fusion | flops 63955852 | bytes 4340304 | tf_op jit(solution)/shard_map/shqk,sqhe->skhe/dot_general | solution.py:58
  147.7 6.0 %fusion.74 = (bf16[12,64]{1,0:T(8,128)(2,1)S(1)}, bf16[1,197,12,64]{1,3,2,0:T(8,128)(2,1)}) fusion(bf16[197,12,64]{0,2,1:T(8,128)(2,1)S(1)} %bitcast.115, f32[12,197,197]{1,2,0:T(8,128)} %fusion.80, f32[12,197]{1,0:T(8,128)S(1)} %log_add_fusion, f32[12,197,197]{1,2,0:T(8,128)} %copy-done.1), kind=kOutput, calls=%fused_computation.129 | convolution fusion | flops 64106380 | bytes 4341840 | tf_op jit(solution)/shard_map/shqk,skhe->sqhe/dot_general | solution.py:58
  153.8 4.6 %multiply_reduce_fusion.3 = (bf16[768]{0:T(1024)(128)(2,1)S(1)}, f32[197]{0:T(256)S(1)}, f32[197]{0:T(256)S(1)}, bf16[768]{0:T(1024)(128)(2,1)S(1)}, f32[197,768]{1,0:T(8,128)}) fusion(f32[197]{0:T(256)S(1)} %copy-done.46, f32[197]{0:T(256)S(1)} %broadcast_multiply_fusion.5, f32[1,197,768]{2,0,1:T(1,128)S(1)} %copy-done.7, f32[768]{0:T(1024)S(1)} %get-tuple-element.122, ...), kind=kOutput, calls=%fused_computation.52 | convolution fusion | flops 711871872 | bytes 5666384 | tf_op jit(solution)/shard_map/dot_general | solution.py:54
  158.4 0.2 dynamic-update-slice
  158.6 0.2 dynamic-update-slice.1
  158.8 0.2 dynamic-update-slice.2
  159.1 0.2 dynamic-update-slice.3
  159.3 0.2 dynamic-update-slice.4
  159.5 0.2 dynamic-update-slice.5
  159.7 0.2 dynamic-update-slice.6
  159.9 0.2 dynamic-update-slice.7
  160.1 0.4 dynamic-update-slice.8
  160.5 1.3 add_bitcast_fusion
  161.9 1.4 copy.66
  163.5 4.3 %convolution_convert_fusion.2 = bf16[768,2304]{1,0:T(8,128)(2,1)} fusion(bf16[197,768]{0,1:T(8,128)(2,1)S(1)} %bitcast.135, bf16[197,768]{0,1:T(8,128)(2,1)} %bitcast.137, bf16[197,768]{0,1:T(8,128)(2,1)} %bitcast.139, f32[768]{0:T(1024)S(1)} %copy-done.48, f32[768]{0:T(1024)S(1)} %get-tuple-element.122, f32[1,197,768]{2,0,1:T(1,128)S(1)} %copy-done.7, ...), kind=kOutput, calls=%fused_computation.3 | convolution fusion | flops 702421248 | bytes 5059624 | tf_op jit(solution)/shard_map/dot_general | solution.py:62
  167.8 3.7 %convolution_convert_fusion.1 = bf16[768,3072]{1,0:T(8,128)(2,1)} fusion(bf16[197,3072]{1,0:T(8,128)(2,1)S(1)} %copy-done.18, f32[197,768]{1,0:T(8,128)S(1)} %get-tuple-element.126, f32[768]{0:T(1024)S(1)} %get-tuple-element.116, f32[768]{0:T(1024)S(1)} %get-tuple-element.117, f32[197]{0:T(256)S(1)} %add_rsqrt_fusion, f32[197]{0:T(256)S(1)} %broadcast_multiply_fusion.4), kind=kOutput, calls=%fused_computation.2 | convolution fusion | flops 932678400 | bytes 6541864 | tf_op jit(solution)/shard_map/dot_general | solution.py:62
  171.6 3.7 %convolution_convert_fusion = bf16[3072,768]{1,0:T(8,128)(2,1)} fusion(bf16[197,3072]{1,0:T(8,128)(2,1)S(1)} %copy-done.13, f32[1,197,768]{2,0,1:T(1,128)S(1)} %copy-done.9, f32[]{:T(128)} %bitcast.16), kind=kOutput, calls=%fused_computation.1 | convolution fusion | flops 932224512 | bytes 6534148 | tf_op jit(solution)/shard_map/dot_general | solution.py:62
  175.3 91.9 %shard_map.346 = (f32[24,2304]{1,0:T(8,128)S(1)}, f32[24,768]{1,0:T(8,128)S(1)}, f32[24,3072]{1,0:T(8,128)S(1)}, f32[96,768]{1,0:T(8,128)S(1)}, f32[16,384]{1,0:T(8,128)S(1)}) custom-call(bf16[4,4,2,24,2304]{4,3,2,1,0:T(8,128)(2,1)} %bitcast.107, bf16[4,4,2,24,768]{4,3,2,1,0:T(8,128)(2,1)S(1)} %bitcast.96, bf16[4,4,2,24,3072]{4,3,2,1,0:T(8,128)(2,1)} %bitcast.100, ...), custom_call_target="tpu_custom_call" | custom-call | tf_op jit(solution)/shard_map/pallas_call | solution.py:369
  267.3 0.6 add_multiply_fusion.1
  267.9 0.7 multiply_add_fusion.6
  268.8 2.3 multiply_add_fusion.4
  271.0 1.1 multiply_add_fusion.2
  272.1 1.1 multiply_add_fusion
  (143 shorter events, 1.2 us)
Async XLA Ops:
  0.7 8.2 %copy-start.28 = (f32[73728]{0:T(1024)S(1)}, f32[73728]{0:T(1024)}, u32[]{:S(2)}) copy-start(f32[73728]{0:T(1024)} %param.24) | copy-start | bytes 884740
  0.7 8.1 %copy-start.26 = (f32[73728]{0:T(1024)S(1)}, f32[73728]{0:T(1024)}, u32[]{:S(2)}) copy-start(f32[73728]{0:T(1024)} %param.23) | copy-start | bytes 884740
  5.5 108.9 %copy-start.45 = (f32[197]{0:T(256)}, f32[197]{0:T(256)S(1)}, u32[]{:S(2)}) copy-start(f32[197]{0:T(256)S(1)} %add_rsqrt_fusion.1) | copy-start | bytes 2368
  97.1 5.2 %copy-start = (bf16[4,4,2,296,768]{4,3,2,1,0:T(8,128)(2,1)}, bf16[4,4,2,296,768]{4,3,2,1,0:T(8,128)(2,1)S(1)}, u32[]{:S(2)}) copy-start(bf16[4,4,2,296,768]{4,3,2,1,0:T(8,128)(2,1)S(1)} %shard_map.345) | copy-start | bytes 43646980
  103.1 11.3 %copy-start.47 = (f32[768]{0:T(1024)}, f32[768]{0:T(1024)S(1)}, u32[]{:S(2)}) copy-start(f32[768]{0:T(1024)S(1)} %get-tuple-element.121) | copy-start | bytes 9220
  107.9 6.6 %copy-start.5 = (f32[1,197,768]{2,0,1:T(1,128)S(1)}, f32[1,197,768]{2,0,1:T(1,128)}, u32[]{:S(2)}) copy-start(f32[1,197,768]{2,0,1:T(1,128)} %param.18) | copy-start | bytes 1815556
  114.4 1.1 copy-start.19
  114.4 1.4 copy-start.20
  114.4 1.8 copy-start.21
  117.5 2.3 copy-start.14
  119.2 16.3 %copy-start.1 = (f32[12,197,197]{1,2,0:T(8,128)}, f32[12,197,197]{1,2,0:T(8,128)S(1)}, u32[]{:S(2)}) copy-start(f32[12,197,197]{1,2,0:T(8,128)S(1)} %get-tuple-element.124) | copy-start | bytes 5588500
  119.2 2.1 copy-start.2
  119.2 2.4 copy-start.6
  119.7 2.7 copy-start.24
  119.7 2.7 copy-start.25
  120.4 2.1 copy-start.11
  120.4 2.5 copy-start.22
  120.4 2.8 %copy-start.23 = (bf16[32,24,768]{2,1,0:T(8,128)(2,1)S(1)}, bf16[32,24,768]{2,1,0:T(8,128)(2,1)}, u32[]{:S(2)}) copy-start(bf16[32,24,768]{2,1,0:T(8,128)(2,1)} %get-tuple-element.102) | copy-start | bytes 3538948
  121.7 2.9 %slice-start = ((s8[4718592]{0:T(1024)(128)(4,1)}), s8[4194304]{0:T(1024)(128)(4,1)S(1)}, s32[]{:S(2)}) async-start(s8[4718592]{0:T(1024)(128)(4,1)} %bitcast.103), calls=%async_computation | async-start | bytes 8388608
  123.2 1.4 copy-start.8
  123.2 1.6 slice-start.1
  124.5 2.5 copy-start.12
  124.8 2.3 copy-start.49
  127.1 2.7 copy-start.17
  132.3 1.3 copy-start.3
  137.9 1.8 copy-start.10
  138.0 3.7 %copy-start.16 = (bf16[197,768]{0,1:T(8,128)(2,1)S(1)}, bf16[197,768]{0,1:T(8,128)(2,1)}, u32[]{:S(2)}) copy-start(bf16[197,768]{0,1:T(8,128)(2,1)} %copy.56) | copy-start | bytes 907780
  141.7 5.9 %copy-start.15 = (bf16[197,768]{0,1:T(8,128)(2,1)S(1)}, bf16[197,768]{0,1:T(8,128)(2,1)}, u32[]{:S(2)}) copy-start(bf16[197,768]{0,1:T(8,128)(2,1)} %copy-done.14) | copy-start | bytes 907780
  147.6 6.1 %copy-start.7 = (f32[1,197,768]{2,0,1:T(1,128)S(1)}, f32[1,197,768]{2,0,1:T(1,128)}, u32[]{:S(2)}) copy-start(f32[1,197,768]{2,0,1:T(1,128)} %param.18) | copy-start | bytes 1815556
  147.7 6.1 %copy-start.46 = (f32[197]{0:T(256)S(1)}, f32[197]{0:T(256)}, u32[]{:S(2)}) copy-start(f32[197]{0:T(256)} %copy-done.45) | copy-start | bytes 2368
  153.7 5.7 %copy-start.53 = (bf16[768]{0:T(1024)(128)(2,1)S(1)}, bf16[768]{0:T(1024)(128)(2,1)}, u32[]{:S(2)}) copy-start(bf16[768]{0:T(1024)(128)(2,1)} %get-tuple-element.76) | copy-start | bytes 4612
  153.7 5.9 %copy-start.52 = (bf16[768]{0:T(1024)(128)(2,1)S(1)}, bf16[768]{0:T(1024)(128)(2,1)}, u32[]{:S(2)}) copy-start(bf16[768]{0:T(1024)(128)(2,1)} %get-tuple-element.82) | copy-start | bytes 4612
  153.8 6.8 %copy-start.4 = (f32[197,768]{1,0:T(8,128)S(1)}, f32[197,768]{1,0:T(8,128)}, u32[]{:S(2)}) copy-start(f32[197,768]{1,0:T(8,128)} %copy-done.3) | copy-start | bytes 1815556
  158.4 5.1 %copy-start.34 = (bf16[1,197,12,64]{1,3,2,0:T(8,128)(2,1)S(1)}, bf16[1,197,12,64]{1,3,2,0:T(8,128)(2,1)}, u32[]{:S(2)}) copy-start(bf16[1,197,12,64]{1,3,2,0:T(8,128)(2,1)} %get-tuple-element.112) | copy-start | bytes 907780
  158.4 5.1 %copy-start.48 = (f32[768]{0:T(1024)S(1)}, f32[768]{0:T(1024)}, u32[]{:S(2)}) copy-start(f32[768]{0:T(1024)} %copy-done.47) | copy-start | bytes 9220
  163.5 4.3 %copy-start.18 = (bf16[197,3072]{1,0:T(8,128)(2,1)S(1)}, bf16[197,3072]{1,0:T(8,128)(2,1)}, u32[]{:S(2)}) copy-start(bf16[197,3072]{1,0:T(8,128)(2,1)} %copy-done.17) | copy-start | bytes 3631108
  167.8 3.7 %copy-start.9 = (f32[1,197,768]{2,0,1:T(1,128)S(1)}, f32[1,197,768]{2,0,1:T(1,128)}, u32[]{:S(2)}) copy-start(f32[1,197,768]{2,0,1:T(1,128)} %param.19) | copy-start | bytes 1815556
  167.8 3.7 %copy-start.13 = (bf16[197,3072]{1,0:T(8,128)(2,1)S(1)}, bf16[197,3072]{1,0:T(8,128)(2,1)}, u32[]{:S(2)}) copy-start(bf16[197,3072]{1,0:T(8,128)(2,1)} %copy-done.12) | copy-start | bytes 3631108
  175.2 92.0 %copy-start.44 = (f32[288]{0:T(512)S(1)}, f32[288]{0:T(512)}, u32[]{:S(2)}) copy-start(f32[288]{0:T(512)} %param.25) | copy-start | bytes 3460
  175.2 92.0 %copy-start.50 = (f32[288]{0:T(512)S(1)}, f32[288]{0:T(512)}, u32[]{:S(2)}) copy-start(f32[288]{0:T(512)} %param.30) | copy-start | bytes 3460
  175.2 92.0 %copy-start.51 = (f32[288]{0:T(512)S(1)}, f32[288]{0:T(512)}, u32[]{:S(2)}) copy-start(f32[288]{0:T(512)} %param.35) | copy-start | bytes 3460
  175.2 92.7 %copy-start.35 = (f32[18432]{0:T(1024)S(1)}, f32[18432]{0:T(1024)}, u32[]{:S(2)}) copy-start(f32[18432]{0:T(1024)} %param.22) | copy-start | bytes 221188
  175.2 92.7 %copy-start.41 = (f32[18432]{0:T(1024)S(1)}, f32[18432]{0:T(1024)}, u32[]{:S(2)}) copy-start(f32[18432]{0:T(1024)} %param.27) | copy-start | bytes 221188
  175.2 92.7 %copy-start.42 = (f32[18432]{0:T(1024)S(1)}, f32[18432]{0:T(1024)}, u32[]{:S(2)}) copy-start(f32[18432]{0:T(1024)} %param.32) | copy-start | bytes 221188
  267.1 1.6 copy-start.33
  267.1 3.9 %copy-start.27 = (f32[73728]{0:T(1024)S(1)}, f32[73728]{0:T(1024)}, u32[]{:S(2)}) copy-start(f32[73728]{0:T(1024)} %param.23) | copy-start | bytes 884740
  267.1 3.9 %copy-start.37 = (f32[73728]{0:T(1024)S(1)}, f32[73728]{0:T(1024)}, u32[]{:S(2)}) copy-start(f32[73728]{0:T(1024)} %param.28) | copy-start | bytes 884740
  267.2 3.9 %copy-start.38 = (f32[73728]{0:T(1024)S(1)}, f32[73728]{0:T(1024)}, u32[]{:S(2)}) copy-start(f32[73728]{0:T(1024)} %param.33) | copy-start | bytes 884740
  267.2 4.9 %copy-start.32 = (f32[55296]{0:T(1024)}, f32[55296]{0:T(1024)S(1)}, u32[]{:S(2)}) copy-start(f32[55296]{0:T(1024)S(1)} %reshape.315) | copy-start | bytes 663556
  267.3 4.8 %copy-start.43 = (f32[288]{0:T(512)}, f32[288]{0:T(512)S(1)}, u32[]{:S(2)}) copy-start(f32[288]{0:T(512)S(1)} %slice_reduce_fusion) | copy-start | bytes 3460
  267.9 4.2 %copy-start.36 = (f32[18432]{0:T(1024)}, f32[18432]{0:T(1024)S(1)}, u32[]{:S(2)}) copy-start(f32[18432]{0:T(1024)S(1)} %reshape.316) | copy-start | bytes 221188
  268.6 3.5 %copy-start.29 = (f32[73728]{0:T(1024)S(1)}, f32[73728]{0:T(1024)}, u32[]{:S(2)}) copy-start(f32[73728]{0:T(1024)} %param.24) | copy-start | bytes 884740
  268.6 3.5 %copy-start.39 = (f32[73728]{0:T(1024)S(1)}, f32[73728]{0:T(1024)}, u32[]{:S(2)}) copy-start(f32[73728]{0:T(1024)} %param.29) | copy-start | bytes 884740
  268.7 3.5 %copy-start.40 = (f32[73728]{0:T(1024)S(1)}, f32[73728]{0:T(1024)}, u32[]{:S(2)}) copy-start(f32[73728]{0:T(1024)} %param.34) | copy-start | bytes 884740
  268.7 4.5 %copy-start.30 = (f32[73728]{0:T(1024)}, f32[73728]{0:T(1024)S(1)}, u32[]{:S(2)}) copy-start(f32[73728]{0:T(1024)S(1)} %reshape.318) | copy-start | bytes 884740
  268.7 4.4 %copy-start.31 = (f32[3,24,8,128]{3,1,2,0:T(8,128)}, f32[3,24,8,128]{3,1,2,0:T(8,128)S(1)}, u32[]{:S(2)}) copy-start(f32[3,24,8,128]{3,1,2,0:T(8,128)S(1)} %copy.73) | copy-start | bytes 884740
